TPU v7x, 512 devices: a whole 4x8x8 slice. The times are simulated.
512 devices in a mesh: gx: 16 (over y, core), gy: 8 (over z_hi, x), gz: 4 (over z_lo).
Axes of the slice: x: 4, y: 8, z: 8 (z_hi: 2, z_lo: 4; z = z_hi * 4 + z_lo), core: 2. Of those that a mesh axis runs over, the one named last changes fastest.
Arguments:
- adjoint_final: float32 [3, 512, 64, 512], P(None, 'gx', 'gy', 'gz'), may hold values from -6 to 6
- velocity: float32 [3, 512, 64, 512], P(None, ('gx', 'gy', 'gz')), may hold values from -0.15 to 0.15
- diffusivity: float32 [3, 512, 64, 512], P(None, 'gx', 'gy', 'gz'), may hold values from 0.01 to 0.04
- upwind_side: int32 [3, 512, 64, 512], P(None, 'gx', 'gy', 'gz'), may hold values 0 or 1
- wall_mask: int32 [512, 64, 512], P('gx', 'gy', 'gz'), may hold values 0 or 1
Outputs:
- adjoint_initial: float32 [3, 512, 64, 512], P(None, 'gx', 'gy', 'gz')
All inputs are finite; a program needn't handle non-finite values. No bound on the sum of `upwind_side` or of `wall_mask` on one device may be relied on, other than what follows from the above.
Results may differ from a plain program's by a relative error of at most 0.00002.
Values sent between devices are 32-bit elements; how exact they have to be, the bound alone decides.
A program may use at most 128 MiB of HBM per device.

v0:
```python
import jax
import jax.numpy as jnp
from jax import lax
from jax.sharding import PartitionSpec as P

STEPS = 5


step_scale = 0.8
half_scale = 0.4


def with_halo(cells, sides, width):
    for axis, dim in sides:
        count = lax.axis_size(axis)
        ends = count - 1
        head = lax.slice_in_dim(cells, 0, width, axis=dim)
        tail = lax.slice_in_dim(cells, cells.shape[dim] - width, cells.shape[dim], axis=dim)
        cells = jnp.concatenate(
            [
                lax.ppermute(tail, axis, [(i, (i + 1) % count) for i in range(ends)]),
                cells,
                lax.ppermute(head, axis, [((i + 1) % count, i) for i in range(ends)]),
            ],
            axis=dim,
        )
    return cells


def offset_view(extended, dim, step):
    parts = [slice(None), slice(1, -1), slice(1, -1), slice(1, -1)]
    extent = extended.shape[dim]
    parts[dim] = slice(1 + step, extent - 1 + step)
    return extended[tuple(parts)]


def advance(extended, coeffs, keep):
    center = extended[:, 1:-1, 1:-1, 1:-1]
    change = jnp.zeros_like(center)
    for which in range(3):
        above = offset_view(extended, which + 1, 1)
        below = offset_view(extended, which + 1, -1)
        change = (
            change + coeffs[2 * which] * (above - center) + coeffs[2 * which + 1] * (below - center)
        )
    return keep * (center + change)


def single_step(adjoint, coeffs, keep):
    extended = with_halo(adjoint, (("gx", 1), ("gy", 2), ("gz", 3)), 1)
    return advance(extended, coeffs, keep)


def local(adjoint_final, velocity, diffusivity, upwind_side, wall_mask):
    cells_y = adjoint_final.shape[2]
    cells_z = adjoint_final.shape[3]
    slab = velocity.shape[1]
    groups_y = lax.axis_size("gy")
    groups_z = lax.axis_size("gz")
    blocks = velocity.reshape(3, slab, groups_y, cells_y, groups_z, cells_z)
    blocks = blocks.transpose(0, 1, 2, 4, 3, 5).reshape(
        3, slab, groups_y * groups_z * cells_y, cells_z
    )
    brick = lax.all_to_all(blocks, ("gy", "gz"), split_axis=2, concat_axis=1, tiled=True)
    speed = jnp.abs(brick)
    side = upwind_side.astype(jnp.float32)
    forward = step_scale * speed * side
    backward = step_scale * speed * (1.0 - side)
    keep = (1 - wall_mask).astype(jnp.float32)[None]
    fields = jnp.concatenate([backward, diffusivity], axis=0)
    extended = with_halo(fields, (("gx", 1), ("gy", 2), ("gz", 3)), 1)
    brick_index = (lax.axis_index("gx"), lax.axis_index("gy"), lax.axis_index("gz"))
    brick_count = (lax.axis_size("gx"), lax.axis_size("gy"), lax.axis_size("gz"))
    coeffs = []
    for which in range(3):
        extent = adjoint_final.shape[which + 1]
        shape = [1, 1, 1, 1]
        shape[which + 1] = extent
        place = (brick_index[which] * extent + jnp.arange(extent, dtype=jnp.int32)).reshape(shape)
        total = extent * brick_count[which]
        valid_up = (place < total - 1).astype(jnp.float32)
        valid_dn = (place > 0).astype(jnp.float32)
        upper_cells = offset_view(extended, which + 1, 1)
        lower_cells = offset_view(extended, which + 1, -1)
        coeffs.append(
            valid_up * (forward[which : which + 1] + half_scale * (diffusivity + upper_cells[3:6]))
        )
        coeffs.append(
            valid_dn
            * (lower_cells[which : which + 1] + half_scale * (lower_cells[3:6] + diffusivity))
        )
    adjoint = adjoint_final
    for step in range(STEPS):
        adjoint = single_step(adjoint, coeffs, keep)
    return adjoint


def solution(mesh):
    return jax.shard_map(
        local,
        mesh=mesh,
        in_specs=(
            P(None, "gx", "gy", "gz"),
            P(None, ("gx", "gy", "gz"), None, None),
            P(None, "gx", "gy", "gz"),
            P(None, "gx", "gy", "gz"),
            P("gx", "gy", "gz"),
        ),
        out_specs=P(None, "gx", "gy", "gz"),
        check_vma=False,
    )
```

profile of v0, /device:TPU:31, one launch (start us, length us, event | category | flops | bytes accessed | tf_op | source)
XLA Modules:
  0.0 259.2 jit_solution(13228813189329289856)
XLA Ops:
  0.8 2.6 collective-permute-start.1
  3.4 4.3 %collective-permute-start.3 = (f32[3,1,8,128]{3,2,1,0:T(8,128)S(1)}, f32[3,1,8,128]{3,2,1,0:T(8,128)S(1)}, u32[]{:S(2)}, u32[]{:S(2)}) collective-permute-start(f32[3,1,8,128]{3,2,1,0:T(8,128)S(1)} %get-tuple-element.55), channel_id=1, source_target_pairs={{0,32},{32,64},{64,96},{96,128},{128,160},{160,192},{192,224},{224... | collective-permute-start | bytes 36872 | tf_op jit(solution)/shard_map/ppermute | solution.py:21
  7.7 2.1 copy.104
  9.8 13.0 %all-to-all-start = ((f32[3,1,256,128]{3,1,0,2:T(1,128)}), f32[3,1,256,128]{3,1,0,2:T(1,128)S(1)}, u32[]{:S(2)}, u32[]{:S(2)}) async-start(f32[3,1,256,128]{3,1,0,2:T(1,128)} %copy.104), calls=%async_computation | async-start | bytes 786432 | tf_op jit(solution)/shard_map/all_to_all | solution.py:64
  23.6 7.1 %collective-permute-start.7 = (f32[3,34,1,128]{3,2,1,0:T(1,128)S(1)}, f32[3,34,1,128]{3,2,1,0:T(1,128)S(1)}, u32[]{:S(2)}, u32[]{:S(2)}) collective-permute-start(f32[3,34,1,128]{3,2,1,0:T(1,128)S(1)} %get-tuple-element.41), channel_id=1, source_target_pairs={{0,4},{4,8},{8,12},{12,16},{16,20},{20,24},{24,28},{1,5},{5,9},{9,... | collective-permute-start | bytes 156680 | tf_op jit(solution)/shard_map/ppermute | solution.py:21
  33.3 8.4 %collective-permute-done.5 = f32[3,34,1,128]{3,2,1,0:T(1,128)S(1)} collective-permute-done((f32[3,34,1,128]{3,2,1,0:T(1,128)S(1)}, f32[3,34,1,128]{3,2,1,0:T(1,128)S(1)}, u32[]{:S(2)}, u32[]{:S(2)}) %collective-permute-start.5) | collective-permute-done | bytes 52256 | tf_op jit(solution)/shard_map/ppermute | solution.py:23
  42.7 4.4 %collective-permute-start.2 = (f32[6,1,8,128]{3,2,1,0:T(8,128)S(1)}, f32[6,1,8,128]{3,2,1,0:T(8,128)S(1)}, u32[]{:S(2)}, u32[]{:S(2)}) collective-permute-start(f32[6,1,8,128]{3,2,1,0:T(8,128)S(1)} %get-tuple-element.29), channel_id=1, source_target_pairs={{0,32},{32,64},{64,96},{96,128},{128,160},{160,192},{192,224},{224... | collective-permute-start | bytes 73736 | tf_op jit(solution)/shard_map/ppermute | solution.py:21
  52.3 3.1 %collective-permute-start.11 = (f32[3,34,10,1]{1,2,3,0:T(8,128)S(1)}, f32[3,34,10,1]{1,2,3,0:T(8,128)S(1)}, u32[]{:S(2)}, u32[]{:S(2)}) collective-permute-start(f32[3,34,10,1]{1,2,3,0:T(8,128)S(1)} %copy.118), channel_id=1, source_target_pairs={{0,1},{1,2},{2,3},{4,5},{5,6},{6,7},{8,9},{9,10},{10,11},{12,13},{... | collective-permute-start | bytes 12248 | tf_op jit(solution)/shard_map/ppermute | solution.py:21
  58.9 9.4 %collective-permute-start.6 = (f32[6,34,1,128]{3,1,2,0:T(8,128)S(1)}, f32[6,34,1,128]{3,1,2,0:T(8,128)S(1)}, u32[]{:S(2)}, u32[]{:S(2)}) collective-permute-start(f32[6,34,1,128]{3,1,2,0:T(8,128)S(1)} %copy.108), channel_id=1, source_target_pairs={{0,4},{4,8},{8,12},{12,16},{16,20},{20,24},{24,28},{1,5},{5,9},{9,... | collective-permute-start | bytes 313352 | tf_op jit(solution)/shard_map/ppermute | solution.py:21
  76.0 5.3 %collective-permute-start.10 = (f32[6,34,10,1]{1,0,3,2:T(8,128)S(1)}, f32[6,34,10,1]{1,0,3,2:T(8,128)S(1)}, u32[]{:S(2)}, u32[]{:S(2)}) collective-permute-start(f32[6,34,10,1]{1,0,3,2:T(8,128)S(1)} %copy.116), channel_id=1, source_target_pairs={{0,1},{1,2},{2,3},{4,5},{5,6},{6,7},{8,9},{9,10},{10,11},{12,13},{... | collective-permute-start | bytes 24488 | tf_op jit(solution)/shard_map/ppermute | solution.py:21
  89.5 5.3 %fusion.80 = (f32[3,32,8,128]{3,2,1,0:T(8,128)S(1)}, f32[3,32,8,128]{3,2,1,0:T(8,128)S(1)}, f32[3,32,8,128]{3,2,1,0:T(8,128)S(1)}, f32[3,32,8,128]{3,2,1,0:T(8,1...) fusion(f32[3,32,8,128]{3,2,1,0:T(8,128)} %param.5, ...), kind=kLoop, calls=%fused_computation.159 | loop fusion | flops 7569408 | bytes 5680352 | tf_op jit(solution)/shard_map/mul | solution.py:46
  94.8 6.1 %collective-permute-start.13 = (f32[3,1,8,128]{3,2,1,0:T(8,128)S(1)}, f32[3,1,8,128]{3,2,1,0:T(8,128)S(1)}, u32[]{:S(2)}, u32[]{:S(2)}) collective-permute-start(f32[3,1,8,128]{3,2,1,0:T(8,128)S(1)} %get-tuple-element.49), channel_id=1, source_target_pairs={{0,32},{32,64},{64,96},{96,128},{128,160},{160,192},{192,224},{224... | collective-permute-start | bytes 36872 | tf_op jit(solution)/shard_map/ppermute | solution.py:21
  102.8 4.3 %collective-permute-done.12 = f32[3,1,8,128]{3,2,1,0:T(8,128)S(1)} collective-permute-done((f32[3,1,8,128]{3,2,1,0:T(8,128)S(1)}, f32[3,1,8,128]{3,2,1,0:T(8,128)S(1)}, u32[]{:S(2)}, u32[]{:S(2)}) %collective-permute-start.12) | collective-permute-done | bytes 12320 | tf_op jit(solution)/shard_map/ppermute | solution.py:23
  107.2 9.6 %collective-permute-start.15 = (f32[3,34,1,128]{3,2,1,0:T(1,128)S(1)}, f32[3,34,1,128]{3,2,1,0:T(1,128)S(1)}, u32[]{:S(2)}, u32[]{:S(2)}) collective-permute-start(f32[3,34,1,128]{3,2,1,0:T(1,128)S(1)} %get-tuple-element.39), channel_id=1, source_target_pairs={{0,4},{4,8},{8,12},{12,16},{16,20},{20,24},{24,28},{1,5},{5,9},{9,... | collective-permute-start | bytes 156680 | tf_op jit(solution)/shard_map/ppermute | solution.py:21
  118.8 8.9 %collective-permute-done.14 = f32[3,34,1,128]{3,2,1,0:T(1,128)S(1)} collective-permute-done((f32[3,34,1,128]{3,2,1,0:T(1,128)S(1)}, f32[3,34,1,128]{3,2,1,0:T(1,128)S(1)}, u32[]{:S(2)}, u32[]{:S(2)}) %collective-permute-start.14) | collective-permute-done | bytes 52256 | tf_op jit(solution)/shard_map/ppermute | solution.py:23
  134.0 4.2 %collective-permute-start.17 = (f32[3,34,10,1]{1,2,3,0:T(8,128)S(1)}, f32[3,34,10,1]{1,2,3,0:T(8,128)S(1)}, u32[]{:S(2)}, u32[]{:S(2)}) collective-permute-start(f32[3,34,10,1]{1,2,3,0:T(8,128)S(1)} %copy.122), channel_id=1, source_target_pairs={{0,1},{1,2},{2,3},{4,5},{5,6},{6,7},{8,9},{9,10},{10,11},{12,13},{... | collective-permute-start | bytes 12248 | tf_op jit(solution)/shard_map/ppermute | solution.py:21
  143.0 3.9 %collective-permute-start.19 = (f32[3,1,8,128]{3,2,1,0:T(8,128)S(1)}, f32[3,1,8,128]{3,2,1,0:T(8,128)S(1)}, u32[]{:S(2)}, u32[]{:S(2)}) collective-permute-start(f32[3,1,8,128]{3,2,1,0:T(8,128)S(1)} %get-tuple-element.47), channel_id=1, source_target_pairs={{0,32},{32,64},{64,96},{96,128},{128,160},{160,192},{192,224},{224... | collective-permute-start | bytes 36872 | tf_op jit(solution)/shard_map/ppermute | solution.py:21
  148.8 4.3 %collective-permute-done.18 = f32[3,1,8,128]{3,2,1,0:T(8,128)S(1)} collective-permute-done((f32[3,1,8,128]{3,2,1,0:T(8,128)S(1)}, f32[3,1,8,128]{3,2,1,0:T(8,128)S(1)}, u32[]{:S(2)}, u32[]{:S(2)}) %collective-permute-start.18) | collective-permute-done | bytes 12320 | tf_op jit(solution)/shard_map/ppermute | solution.py:23
  155.1 3.4 %collective-permute-start.20 = (f32[3,34,1,128]{3,2,1,0:T(1,128)S(1)}, f32[3,34,1,128]{3,2,1,0:T(1,128)S(1)}, u32[]{:S(2)}, u32[]{:S(2)}) collective-permute-start(f32[3,34,1,128]{3,2,1,0:T(1,128)S(1)} %get-tuple-element.38), channel_id=1, source_target_pairs={{4,0},{8,4},{12,8},{16,12},{20,16},{24,20},{28,24},{5,1},{9,5},{13... | collective-permute-start | bytes 156680 | tf_op jit(solution)/shard_map/ppermute | solution.py:23
  158.5 7.5 %collective-permute-done.20 = f32[3,34,1,128]{3,2,1,0:T(1,128)S(1)} collective-permute-done((f32[3,34,1,128]{3,2,1,0:T(1,128)S(1)}, f32[3,34,1,128]{3,2,1,0:T(1,128)S(1)}, u32[]{:S(2)}, u32[]{:S(2)}) %collective-permute-start.20) | collective-permute-done | bytes 52256 | tf_op jit(solution)/shard_map/ppermute | solution.py:23
  172.2 4.8 %collective-permute-start.23 = (f32[3,34,10,1]{1,2,3,0:T(8,128)S(1)}, f32[3,34,10,1]{1,2,3,0:T(8,128)S(1)}, u32[]{:S(2)}, u32[]{:S(2)}) collective-permute-start(f32[3,34,10,1]{1,2,3,0:T(8,128)S(1)} %copy.126), channel_id=1, source_target_pairs={{0,1},{1,2},{2,3},{4,5},{5,6},{6,7},{8,9},{9,10},{10,11},{12,13},{... | collective-permute-start | bytes 12248 | tf_op jit(solution)/shard_map/ppermute | solution.py:21
  181.8 3.5 %collective-permute-start.25 = (f32[3,1,8,128]{3,2,1,0:T(8,128)S(1)}, f32[3,1,8,128]{3,2,1,0:T(8,128)S(1)}, u32[]{:S(2)}, u32[]{:S(2)}) collective-permute-start(f32[3,1,8,128]{3,2,1,0:T(8,128)S(1)} %get-tuple-element.45), channel_id=1, source_target_pairs={{0,32},{32,64},{64,96},{96,128},{128,160},{160,192},{192,224},{224... | collective-permute-start | bytes 36872 | tf_op jit(solution)/shard_map/ppermute | solution.py:21
  187.2 4.3 %collective-permute-done.24 = f32[3,1,8,128]{3,2,1,0:T(8,128)S(1)} collective-permute-done((f32[3,1,8,128]{3,2,1,0:T(8,128)S(1)}, f32[3,1,8,128]{3,2,1,0:T(8,128)S(1)}, u32[]{:S(2)}, u32[]{:S(2)}) %collective-permute-start.24) | collective-permute-done | bytes 12320 | tf_op jit(solution)/shard_map/ppermute | solution.py:23
  193.5 3.4 %collective-permute-start.26 = (f32[3,34,1,128]{3,2,1,0:T(1,128)S(1)}, f32[3,34,1,128]{3,2,1,0:T(1,128)S(1)}, u32[]{:S(2)}, u32[]{:S(2)}) collective-permute-start(f32[3,34,1,128]{3,2,1,0:T(1,128)S(1)} %get-tuple-element.36), channel_id=1, source_target_pairs={{4,0},{8,4},{12,8},{16,12},{20,16},{24,20},{28,24},{5,1},{9,5},{13... | collective-permute-start | bytes 156680 | tf_op jit(solution)/shard_map/ppermute | solution.py:23
  196.9 7.5 %collective-permute-done.26 = f32[3,34,1,128]{3,2,1,0:T(1,128)S(1)} collective-permute-done((f32[3,34,1,128]{3,2,1,0:T(1,128)S(1)}, f32[3,34,1,128]{3,2,1,0:T(1,128)S(1)}, u32[]{:S(2)}, u32[]{:S(2)}) %collective-permute-start.26) | collective-permute-done | bytes 52256 | tf_op jit(solution)/shard_map/ppermute | solution.py:23
  210.5 4.6 %collective-permute-start.29 = (f32[3,34,10,1]{1,2,3,0:T(8,128)S(1)}, f32[3,34,10,1]{1,2,3,0:T(8,128)S(1)}, u32[]{:S(2)}, u32[]{:S(2)}) collective-permute-start(f32[3,34,10,1]{1,2,3,0:T(8,128)S(1)} %copy.130), channel_id=1, source_target_pairs={{0,1},{1,2},{2,3},{4,5},{5,6},{6,7},{8,9},{9,10},{10,11},{12,13},{... | collective-permute-start | bytes 12248 | tf_op jit(solution)/shard_map/ppermute | solution.py:21
  219.8 3.5 %collective-permute-start.31 = (f32[3,1,8,128]{3,2,1,0:T(8,128)S(1)}, f32[3,1,8,128]{3,2,1,0:T(8,128)S(1)}, u32[]{:S(2)}, u32[]{:S(2)}) collective-permute-start(f32[3,1,8,128]{3,2,1,0:T(8,128)S(1)} %get-tuple-element.43), channel_id=1, source_target_pairs={{0,32},{32,64},{64,96},{96,128},{128,160},{160,192},{192,224},{224... | collective-permute-start | bytes 36872 | tf_op jit(solution)/shard_map/ppermute | solution.py:21
  225.3 4.3 %collective-permute-done.30 = f32[3,1,8,128]{3,2,1,0:T(8,128)S(1)} collective-permute-done((f32[3,1,8,128]{3,2,1,0:T(8,128)S(1)}, f32[3,1,8,128]{3,2,1,0:T(8,128)S(1)}, u32[]{:S(2)}, u32[]{:S(2)}) %collective-permute-start.30) | collective-permute-done | bytes 12320 | tf_op jit(solution)/shard_map/ppermute | solution.py:23
  231.6 3.4 %collective-permute-start.32 = (f32[3,34,1,128]{3,2,1,0:T(1,128)S(1)}, f32[3,34,1,128]{3,2,1,0:T(1,128)S(1)}, u32[]{:S(2)}, u32[]{:S(2)}) collective-permute-start(f32[3,34,1,128]{3,2,1,0:T(1,128)S(1)} %get-tuple-element.34), channel_id=1, source_target_pairs={{4,0},{8,4},{12,8},{16,12},{20,16},{24,20},{28,24},{5,1},{9,5},{13... | collective-permute-start | bytes 156680 | tf_op jit(solution)/shard_map/ppermute | solution.py:23
  235.0 7.5 %collective-permute-done.32 = f32[3,34,1,128]{3,2,1,0:T(1,128)S(1)} collective-permute-done((f32[3,34,1,128]{3,2,1,0:T(1,128)S(1)}, f32[3,34,1,128]{3,2,1,0:T(1,128)S(1)}, u32[]{:S(2)}, u32[]{:S(2)}) %collective-permute-start.32) | collective-permute-done | bytes 52256 | tf_op jit(solution)/shard_map/ppermute | solution.py:23
  248.5 5.1 %collective-permute-start.35 = (f32[3,34,10,1]{1,2,3,0:T(8,128)S(1)}, f32[3,34,10,1]{1,2,3,0:T(8,128)S(1)}, u32[]{:S(2)}, u32[]{:S(2)}) collective-permute-start(f32[3,34,10,1]{1,2,3,0:T(8,128)S(1)} %copy.134), channel_id=1, source_target_pairs={{0,1},{1,2},{2,3},{4,5},{5,6},{6,7},{8,9},{9,10},{10,11},{12,13},{... | collective-permute-start | bytes 12248 | tf_op jit(solution)/shard_map/ppermute | solution.py:21
  256.4 2.8 %fusion.4 = f32[3,32,8,128]{3,2,1,0:T(8,128)} fusion(f32[3,32,8,128]{3,2,1,0:T(8,128)S(1)} %fusion.23, f32[3,32,8,128]{3,2,1,0:T(8,128)S(1)} %copy-done.4, f32[3,34,10,1]{3,2,1,0:T(8,128)} %copy.135, f32[3,34,1,128]{3,2,1,0:T(1,128)S(1)} %collective-permute-done.32, f32[3,34,1,128]{3,2,1,0:T(1,128)S(1)} %collective-permute-done.33, ...), kind=kLoop, calls=%fused_computation.11 | loop fusion | flops 3637248 | bytes 3413984 | tf_op jit(solution)/shard_map/mul | solution.py:46
  (146 shorter events, 86.7 us)
Async XLA Ops:
  0.8 22.8 %collective-permute-start.1 = (f32[3,1,8,128]{3,2,1,0:T(8,128)S(1)}, f32[3,1,8,128]{3,2,1,0:T(8,128)S(1)}, u32[]{:S(2)}, u32[]{:S(2)}) collective-permute-start(f32[3,1,8,128]{3,2,1,0:T(8,128)S(1)} %get-tuple-element.54), channel_id=1, source_target_pairs={{32,0},{64,32},{96,64},{128,96},{160,128},{192,160},{224,192},{256... | collective-permute-start | bytes 36872 | tf_op jit(solution)/shard_map/ppermute | solution.py:23
  3.4 20.1 %collective-permute-start.3 = (f32[3,1,8,128]{3,2,1,0:T(8,128)S(1)}, f32[3,1,8,128]{3,2,1,0:T(8,128)S(1)}, u32[]{:S(2)}, u32[]{:S(2)}) collective-permute-start(f32[3,1,8,128]{3,2,1,0:T(8,128)S(1)} %get-tuple-element.55), channel_id=1, source_target_pairs={{0,32},{32,64},{64,96},{96,128},{128,160},{160,192},{192,224},{224... | collective-permute-start | bytes 36872 | tf_op jit(solution)/shard_map/ppermute | solution.py:21
  9.8 32.0 %all-to-all-start = ((f32[3,1,256,128]{3,1,0,2:T(1,128)}), f32[3,1,256,128]{3,1,0,2:T(1,128)S(1)}, u32[]{:S(2)}, u32[]{:S(2)}) async-start(f32[3,1,256,128]{3,1,0,2:T(1,128)} %copy.104), calls=%async_computation | async-start | bytes 786432 | tf_op jit(solution)/shard_map/all_to_all | solution.py:64
  23.6 9.7 %collective-permute-start.7 = (f32[3,34,1,128]{3,2,1,0:T(1,128)S(1)}, f32[3,34,1,128]{3,2,1,0:T(1,128)S(1)}, u32[]{:S(2)}, u32[]{:S(2)}) collective-permute-start(f32[3,34,1,128]{3,2,1,0:T(1,128)S(1)} %get-tuple-element.41), channel_id=1, source_target_pairs={{0,4},{4,8},{8,12},{12,16},{16,20},{20,24},{24,28},{1,5},{5,9},{9,... | collective-permute-start | bytes 156680 | tf_op jit(solution)/shard_map/ppermute | solution.py:21
  30.8 10.9 %collective-permute-start.5 = (f32[3,34,1,128]{3,2,1,0:T(1,128)S(1)}, f32[3,34,1,128]{3,2,1,0:T(1,128)S(1)}, u32[]{:S(2)}, u32[]{:S(2)}) collective-permute-start(f32[3,34,1,128]{3,2,1,0:T(1,128)S(1)} %get-tuple-element.42), channel_id=1, source_target_pairs={{4,0},{8,4},{12,8},{16,12},{20,16},{24,20},{28,24},{5,1},{9,5},{13... | collective-permute-start | bytes 156680 | tf_op jit(solution)/shard_map/ppermute | solution.py:23
  42.7 14.0 %collective-permute-start.2 = (f32[6,1,8,128]{3,2,1,0:T(8,128)S(1)}, f32[6,1,8,128]{3,2,1,0:T(8,128)S(1)}, u32[]{:S(2)}, u32[]{:S(2)}) collective-permute-start(f32[6,1,8,128]{3,2,1,0:T(8,128)S(1)} %get-tuple-element.29), channel_id=1, source_target_pairs={{0,32},{32,64},{64,96},{96,128},{128,160},{160,192},{192,224},{224... | collective-permute-start | bytes 73736 | tf_op jit(solution)/shard_map/ppermute | solution.py:21
  47.1 9.6 %collective-permute-start = (f32[6,1,8,128]{3,2,1,0:T(8,128)S(1)}, f32[6,1,8,128]{3,2,1,0:T(8,128)S(1)}, u32[]{:S(2)}, u32[]{:S(2)}) collective-permute-start(f32[6,1,8,128]{3,2,1,0:T(8,128)S(1)} %get-tuple-element.30), channel_id=1, source_target_pairs={{32,0},{64,32},{96,64},{128,96},{160,128},{192,160},{224,192},{256... | collective-permute-start | bytes 73736 | tf_op jit(solution)/shard_map/ppermute | solution.py:23
  52.3 17.9 %collective-permute-start.11 = (f32[3,34,10,1]{1,2,3,0:T(8,128)S(1)}, f32[3,34,10,1]{1,2,3,0:T(8,128)S(1)}, u32[]{:S(2)}, u32[]{:S(2)}) collective-permute-start(f32[3,34,10,1]{1,2,3,0:T(8,128)S(1)} %copy.118), channel_id=1, source_target_pairs={{0,1},{1,2},{2,3},{4,5},{5,6},{6,7},{8,9},{9,10},{10,11},{12,13},{... | collective-permute-start | bytes 12248 | tf_op jit(solution)/shard_map/ppermute | solution.py:21
  55.4 13.4 %collective-permute-start.9 = (f32[3,34,10,1]{1,2,3,0:T(8,128)S(1)}, f32[3,34,10,1]{1,2,3,0:T(8,128)S(1)}, u32[]{:S(2)}, u32[]{:S(2)}) collective-permute-start(f32[3,34,10,1]{1,2,3,0:T(8,128)S(1)} %copy.114), channel_id=1, source_target_pairs={{1,0},{2,1},{3,2},{5,4},{6,5},{7,6},{9,8},{10,9},{11,10},{13,12},{... | collective-permute-start | bytes 12248 | tf_op jit(solution)/shard_map/ppermute | solution.py:23
  56.9 14.6 %collective-permute-start.4 = (f32[6,34,1,128]{3,1,2,0:T(8,128)S(1)}, f32[6,34,1,128]{3,1,2,0:T(8,128)S(1)}, u32[]{:S(2)}, u32[]{:S(2)}) collective-permute-start(f32[6,34,1,128]{3,1,2,0:T(8,128)S(1)} %copy.106), channel_id=1, source_target_pairs={{4,0},{8,4},{12,8},{16,12},{20,16},{24,20},{28,24},{5,1},{9,5},{13... | collective-permute-start | bytes 313352 | tf_op jit(solution)/shard_map/ppermute | solution.py:23
  58.9 12.8 %collective-permute-start.6 = (f32[6,34,1,128]{3,1,2,0:T(8,128)S(1)}, f32[6,34,1,128]{3,1,2,0:T(8,128)S(1)}, u32[]{:S(2)}, u32[]{:S(2)}) collective-permute-start(f32[6,34,1,128]{3,1,2,0:T(8,128)S(1)} %copy.108), channel_id=1, source_target_pairs={{0,4},{4,8},{8,12},{12,16},{16,20},{20,24},{24,28},{1,5},{5,9},{9,... | collective-permute-start | bytes 313352 | tf_op jit(solution)/shard_map/ppermute | solution.py:21
  76.0 8.1 %collective-permute-start.10 = (f32[6,34,10,1]{1,0,3,2:T(8,128)S(1)}, f32[6,34,10,1]{1,0,3,2:T(8,128)S(1)}, u32[]{:S(2)}, u32[]{:S(2)}) collective-permute-start(f32[6,34,10,1]{1,0,3,2:T(8,128)S(1)} %copy.116), channel_id=1, source_target_pairs={{0,1},{1,2},{2,3},{4,5},{5,6},{6,7},{8,9},{9,10},{10,11},{12,13},{... | collective-permute-start | bytes 24488 | tf_op jit(solution)/shard_map/ppermute | solution.py:21
  94.8 8.0 %collective-permute-start.13 = (f32[3,1,8,128]{3,2,1,0:T(8,128)S(1)}, f32[3,1,8,128]{3,2,1,0:T(8,128)S(1)}, u32[]{:S(2)}, u32[]{:S(2)}) collective-permute-start(f32[3,1,8,128]{3,2,1,0:T(8,128)S(1)} %get-tuple-element.49), channel_id=1, source_target_pairs={{0,32},{32,64},{64,96},{96,128},{128,160},{160,192},{192,224},{224... | collective-permute-start | bytes 36872 | tf_op jit(solution)/shard_map/ppermute | solution.py:21
  100.9 6.2 %collective-permute-start.12 = (f32[3,1,8,128]{3,2,1,0:T(8,128)S(1)}, f32[3,1,8,128]{3,2,1,0:T(8,128)S(1)}, u32[]{:S(2)}, u32[]{:S(2)}) collective-permute-start(f32[3,1,8,128]{3,2,1,0:T(8,128)S(1)} %get-tuple-element.50), channel_id=1, source_target_pairs={{32,0},{64,32},{96,64},{128,96},{160,128},{192,160},{224,192},{256... | collective-permute-start | bytes 36872 | tf_op jit(solution)/shard_map/ppermute | solution.py:23
  107.2 11.6 %collective-permute-start.15 = (f32[3,34,1,128]{3,2,1,0:T(1,128)S(1)}, f32[3,34,1,128]{3,2,1,0:T(1,128)S(1)}, u32[]{:S(2)}, u32[]{:S(2)}) collective-permute-start(f32[3,34,1,128]{3,2,1,0:T(1,128)S(1)} %get-tuple-element.39), channel_id=1, source_target_pairs={{0,4},{4,8},{8,12},{12,16},{16,20},{20,24},{24,28},{1,5},{5,9},{9,... | collective-permute-start | bytes 156680 | tf_op jit(solution)/shard_map/ppermute | solution.py:21
  116.8 10.9 %collective-permute-start.14 = (f32[3,34,1,128]{3,2,1,0:T(1,128)S(1)}, f32[3,34,1,128]{3,2,1,0:T(1,128)S(1)}, u32[]{:S(2)}, u32[]{:S(2)}) collective-permute-start(f32[3,34,1,128]{3,2,1,0:T(1,128)S(1)} %get-tuple-element.40), channel_id=1, source_target_pairs={{4,0},{8,4},{12,8},{16,12},{20,16},{24,20},{28,24},{5,1},{9,5},{13... | collective-permute-start | bytes 156680 | tf_op jit(solution)/shard_map/ppermute | solution.py:23
  131.1 7.0 %collective-permute-start.16 = (f32[3,34,10,1]{1,2,3,0:T(8,128)S(1)}, f32[3,34,10,1]{1,2,3,0:T(8,128)S(1)}, u32[]{:S(2)}, u32[]{:S(2)}) collective-permute-start(f32[3,34,10,1]{1,2,3,0:T(8,128)S(1)} %copy.120), channel_id=1, source_target_pairs={{1,0},{2,1},{3,2},{5,4},{6,5},{7,6},{9,8},{10,9},{11,10},{13,12},{... | collective-permute-start | bytes 12248 | tf_op jit(solution)/shard_map/ppermute | solution.py:23
  134.0 5.5 %collective-permute-start.17 = (f32[3,34,10,1]{1,2,3,0:T(8,128)S(1)}, f32[3,34,10,1]{1,2,3,0:T(8,128)S(1)}, u32[]{:S(2)}, u32[]{:S(2)}) collective-permute-start(f32[3,34,10,1]{1,2,3,0:T(8,128)S(1)} %copy.122), channel_id=1, source_target_pairs={{0,1},{1,2},{2,3},{4,5},{5,6},{6,7},{8,9},{9,10},{10,11},{12,13},{... | collective-permute-start | bytes 12248 | tf_op jit(solution)/shard_map/ppermute | solution.py:21
  143.0 5.9 %collective-permute-start.19 = (f32[3,1,8,128]{3,2,1,0:T(8,128)S(1)}, f32[3,1,8,128]{3,2,1,0:T(8,128)S(1)}, u32[]{:S(2)}, u32[]{:S(2)}) collective-permute-start(f32[3,1,8,128]{3,2,1,0:T(8,128)S(1)} %get-tuple-element.47), channel_id=1, source_target_pairs={{0,32},{32,64},{64,96},{96,128},{128,160},{160,192},{192,224},{224... | collective-permute-start | bytes 36872 | tf_op jit(solution)/shard_map/ppermute | solution.py:21
  146.9 6.2 %collective-permute-start.18 = (f32[3,1,8,128]{3,2,1,0:T(8,128)S(1)}, f32[3,1,8,128]{3,2,1,0:T(8,128)S(1)}, u32[]{:S(2)}, u32[]{:S(2)}) collective-permute-start(f32[3,1,8,128]{3,2,1,0:T(8,128)S(1)} %get-tuple-element.48), channel_id=1, source_target_pairs={{32,0},{64,32},{96,64},{128,96},{160,128},{192,160},{224,192},{256... | collective-permute-start | bytes 36872 | tf_op jit(solution)/shard_map/ppermute | solution.py:23
  155.1 10.9 %collective-permute-start.20 = (f32[3,34,1,128]{3,2,1,0:T(1,128)S(1)}, f32[3,34,1,128]{3,2,1,0:T(1,128)S(1)}, u32[]{:S(2)}, u32[]{:S(2)}) collective-permute-start(f32[3,34,1,128]{3,2,1,0:T(1,128)S(1)} %get-tuple-element.38), channel_id=1, source_target_pairs={{4,0},{8,4},{12,8},{16,12},{20,16},{24,20},{28,24},{5,1},{9,5},{13... | collective-permute-start | bytes 156680 | tf_op jit(solution)/shard_map/ppermute | solution.py:23
  169.3 7.7 %collective-permute-start.22 = (f32[3,34,10,1]{1,2,3,0:T(8,128)S(1)}, f32[3,34,10,1]{1,2,3,0:T(8,128)S(1)}, u32[]{:S(2)}, u32[]{:S(2)}) collective-permute-start(f32[3,34,10,1]{1,2,3,0:T(8,128)S(1)} %copy.124), channel_id=1, source_target_pairs={{1,0},{2,1},{3,2},{5,4},{6,5},{7,6},{9,8},{10,9},{11,10},{13,12},{... | collective-permute-start | bytes 12248 | tf_op jit(solution)/shard_map/ppermute | solution.py:23
  172.2 6.1 %collective-permute-start.23 = (f32[3,34,10,1]{1,2,3,0:T(8,128)S(1)}, f32[3,34,10,1]{1,2,3,0:T(8,128)S(1)}, u32[]{:S(2)}, u32[]{:S(2)}) collective-permute-start(f32[3,34,10,1]{1,2,3,0:T(8,128)S(1)} %copy.126), channel_id=1, source_target_pairs={{0,1},{1,2},{2,3},{4,5},{5,6},{6,7},{8,9},{9,10},{10,11},{12,13},{... | collective-permute-start | bytes 12248 | tf_op jit(solution)/shard_map/ppermute | solution.py:21
  185.3 6.2 %collective-permute-start.24 = (f32[3,1,8,128]{3,2,1,0:T(8,128)S(1)}, f32[3,1,8,128]{3,2,1,0:T(8,128)S(1)}, u32[]{:S(2)}, u32[]{:S(2)}) collective-permute-start(f32[3,1,8,128]{3,2,1,0:T(8,128)S(1)} %get-tuple-element.46), channel_id=1, source_target_pairs={{32,0},{64,32},{96,64},{128,96},{160,128},{192,160},{224,192},{256... | collective-permute-start | bytes 36872 | tf_op jit(solution)/shard_map/ppermute | solution.py:23
  193.5 10.9 %collective-permute-start.26 = (f32[3,34,1,128]{3,2,1,0:T(1,128)S(1)}, f32[3,34,1,128]{3,2,1,0:T(1,128)S(1)}, u32[]{:S(2)}, u32[]{:S(2)}) collective-permute-start(f32[3,34,1,128]{3,2,1,0:T(1,128)S(1)} %get-tuple-element.36), channel_id=1, source_target_pairs={{4,0},{8,4},{12,8},{16,12},{20,16},{24,20},{28,24},{5,1},{9,5},{13... | collective-permute-start | bytes 156680 | tf_op jit(solution)/shard_map/ppermute | solution.py:23
  207.6 7.4 %collective-permute-start.28 = (f32[3,34,10,1]{1,2,3,0:T(8,128)S(1)}, f32[3,34,10,1]{1,2,3,0:T(8,128)S(1)}, u32[]{:S(2)}, u32[]{:S(2)}) collective-permute-start(f32[3,34,10,1]{1,2,3,0:T(8,128)S(1)} %copy.128), channel_id=1, source_target_pairs={{1,0},{2,1},{3,2},{5,4},{6,5},{7,6},{9,8},{10,9},{11,10},{13,12},{... | collective-permute-start | bytes 12248 | tf_op jit(solution)/shard_map/ppermute | solution.py:23
  210.5 5.9 %collective-permute-start.29 = (f32[3,34,10,1]{1,2,3,0:T(8,128)S(1)}, f32[3,34,10,1]{1,2,3,0:T(8,128)S(1)}, u32[]{:S(2)}, u32[]{:S(2)}) collective-permute-start(f32[3,34,10,1]{1,2,3,0:T(8,128)S(1)} %copy.130), channel_id=1, source_target_pairs={{0,1},{1,2},{2,3},{4,5},{5,6},{6,7},{8,9},{9,10},{10,11},{12,13},{... | collective-permute-start | bytes 12248 | tf_op jit(solution)/shard_map/ppermute | solution.py:21
  219.8 5.5 %collective-permute-start.31 = (f32[3,1,8,128]{3,2,1,0:T(8,128)S(1)}, f32[3,1,8,128]{3,2,1,0:T(8,128)S(1)}, u32[]{:S(2)}, u32[]{:S(2)}) collective-permute-start(f32[3,1,8,128]{3,2,1,0:T(8,128)S(1)} %get-tuple-element.43), channel_id=1, source_target_pairs={{0,32},{32,64},{64,96},{96,128},{128,160},{160,192},{192,224},{224... | collective-permute-start | bytes 36872 | tf_op jit(solution)/shard_map/ppermute | solution.py:21
  223.4 6.2 %collective-permute-start.30 = (f32[3,1,8,128]{3,2,1,0:T(8,128)S(1)}, f32[3,1,8,128]{3,2,1,0:T(8,128)S(1)}, u32[]{:S(2)}, u32[]{:S(2)}) collective-permute-start(f32[3,1,8,128]{3,2,1,0:T(8,128)S(1)} %get-tuple-element.44), channel_id=1, source_target_pairs={{32,0},{64,32},{96,64},{128,96},{160,128},{192,160},{224,192},{256... | collective-permute-start | bytes 36872 | tf_op jit(solution)/shard_map/ppermute | solution.py:23
  231.6 10.9 %collective-permute-start.32 = (f32[3,34,1,128]{3,2,1,0:T(1,128)S(1)}, f32[3,34,1,128]{3,2,1,0:T(1,128)S(1)}, u32[]{:S(2)}, u32[]{:S(2)}) collective-permute-start(f32[3,34,1,128]{3,2,1,0:T(1,128)S(1)} %get-tuple-element.34), channel_id=1, source_target_pairs={{4,0},{8,4},{12,8},{16,12},{20,16},{24,20},{28,24},{5,1},{9,5},{13... | collective-permute-start | bytes 156680 | tf_op jit(solution)/shard_map/ppermute | solution.py:23
  245.7 8.0 %collective-permute-start.34 = (f32[3,34,10,1]{1,2,3,0:T(8,128)S(1)}, f32[3,34,10,1]{1,2,3,0:T(8,128)S(1)}, u32[]{:S(2)}, u32[]{:S(2)}) collective-permute-start(f32[3,34,10,1]{1,2,3,0:T(8,128)S(1)} %copy.132), channel_id=1, source_target_pairs={{1,0},{2,1},{3,2},{5,4},{6,5},{7,6},{9,8},{10,9},{11,10},{13,12},{... | collective-permute-start | bytes 12248 | tf_op jit(solution)/shard_map/ppermute | solution.py:23
  248.5 6.5 %collective-permute-start.35 = (f32[3,34,10,1]{1,2,3,0:T(8,128)S(1)}, f32[3,34,10,1]{1,2,3,0:T(8,128)S(1)}, u32[]{:S(2)}, u32[]{:S(2)}) collective-permute-start(f32[3,34,10,1]{1,2,3,0:T(8,128)S(1)} %copy.134), channel_id=1, source_target_pairs={{0,1},{1,2},{2,3},{4,5},{5,6},{6,7},{8,9},{9,10},{10,11},{12,13},{... | collective-permute-start | bytes 12248 | tf_op jit(solution)/shard_map/ppermute | solution.py:21
  (23 other events, 408.0 us)
where the time goes:
time: 261 us; the launch traced here: 259 us
  starting transfers between devices  133 us (51%)
  waiting for transfers between devices  58.8 us (23%)
  local copies, waits for them, and re-layouts  47.2 us (18%)
  other arithmetic  19.2 us (7%)
    ppermute x18, starting transfers between devices, with_halo(): lax.ppermute(tail, axis, [(i, (i + 1) % count) for i in range(ends)])  84.6 us
    ppermute x18, waiting for transfers between devices, with_halo(): lax.ppermute(head, axis, [((i + 1) % count, i) for i in range(ends)])  58.7 us
    ppermute x18, starting transfers between devices, with_halo(): lax.ppermute(head, axis, [((i + 1) % count, i) for i in range(ends)])  35.7 us
    slice x13, local copies, waits for them, and re-layouts, with_halo(): head = lax.slice_in_dim(cells, 0, width, axis=dim)  16.6 us
    mul x5, other arithmetic, advance(): return keep * (center + change)  14.2 us
    all_to_all x1, starting transfers between devices, local(): lax.all_to_all(blocks, ('gy', 'gz'), split_axis=2, concat_axis=1, tiled=T...  13 us
    slice x13, local copies, waits for them, and re-layouts, with_halo(): lax.slice_in_dim(cells, cells.shape[dim] - width, cells.shape[dim], axis=...  10.8 us
    ppermute x7, local copies, waits for them, and re-layouts, with_halo(): lax.ppermute(head, axis, [((i + 1) % count, i) for i in range(ends)])  8.83 us
  transfers between devices with their start and end apart: 37, of which 10 were waited for; matrix products, arithmetic and copies ran while one was open for 10% of the time, Pallas kernels for 0%

commit v1 on v0

v1 whole, which is shorter than its diff:
```python
import functools

import jax
import jax.numpy as jnp
from jax import lax
from jax.experimental import pallas as pl
from jax.experimental.pallas import tpu as pltpu
from jax.sharding import PartitionSpec as P

MESH = pl.DeviceIdType.MESH
STEPS = 5
AXES = ("gx", "gy", "gz")
DIF, BACK = STEPS + 1, STEPS + 2

step_scale = 0.8
half_scale = 0.4


def kernel(
    dims, counts,
    adj_h, vel_h, dif_h, side_h, wall_h, out_h,
    A, V, D, S, W, B, C, K, ysnd, yrcv, zsnd, zrcv,
    load_sem, vsend, vrecv, fsend, frecv, out_sem,
):
    SOL, NXL, NYL, NZL = dims
    ny, nz = counts[1], counts[2]
    group = ny * nz
    place = [lax.axis_index(a) for a in AXES]
    has_up = [place[i] < counts[i] - 1 for i in range(3)]
    has_dn = [place[i] > 0 for i in range(3)]
    me = place[1] * nz + place[2]

    loads = [
        pltpu.make_async_copy(adj_h, A.at[0, :, pl.ds(1, NXL)], load_sem.at[0]),
        pltpu.make_async_copy(dif_h, D.at[:, pl.ds(1, NXL)], load_sem.at[1]),
        pltpu.make_async_copy(side_h, S, load_sem.at[2]),
        pltpu.make_async_copy(wall_h, W, load_sem.at[3]),
    ]
    for c in loads:
        c.start()

    barrier = pltpu.get_barrier_semaphore()

    def peer(o):
        p = lax.rem(me + o, group)
        return p // nz, lax.rem(p, nz), p

    @pl.loop(1, group)
    def _(o):
        py, pz, _ = peer(o)
        pl.semaphore_signal(barrier, 1, device_id={"gy": py, "gz": pz}, device_id_type=MESH)

    for cond, d in ((has_up[0], 1), (has_dn[0], -1)):
        @pl.when(cond)
        def _():
            pl.semaphore_signal(barrier, 1, device_id={"gx": place[0] + d}, device_id_type=MESH)

    def face(m, dim, side):
        send, recv = fsend.at[m, dim, side], frecv.at[m, dim, side]
        to = {AXES[dim]: place[dim] + (1 - 2 * side)}
        if dim == 0:
            src_plane, dst_plane = (NXL, 0) if side == 0 else (1, NXL + 1)
            if isinstance(m, int) and m == BACK:
                src, dst = B.at[pl.ds(NXL, 1)], B.at[pl.ds(0, 1)]
            elif isinstance(m, int) and m == DIF:
                src, dst = D.at[:, pl.ds(src_plane, 1)], D.at[:, pl.ds(dst_plane, 1)]
            else:
                src, dst = A.at[m, :, pl.ds(src_plane, 1)], A.at[m, :, pl.ds(dst_plane, 1)]
        elif dim == 1:
            if isinstance(m, int) and m == BACK:
                src, dst = ysnd.at[m, side, pl.ds(0, NXL)], yrcv.at[m, side, pl.ds(0, NXL)]
            else:
                src, dst = ysnd.at[m, side], yrcv.at[m, side]
        else:
            src, dst = zsnd.at[m, side], zrcv.at[m, side]
        return pltpu.make_async_remote_copy(
            src_ref=src, dst_ref=dst, send_sem=send, recv_sem=recv, device_id=to, device_id_type=MESH
        )

    def sides(dim):
        return ((0, has_up[dim], has_dn[dim]), (1, has_dn[dim], has_up[dim]))

    def send_face(m, dim, only=None):
        for side, to, _ in sides(dim):
            if only is None or side == only:
                @pl.when(to)
                def _():
                    face(m, dim, side).start()

    def wait_face(m, dim, only=None):
        for side, _, fro in sides(dim):
            if only is None or side == only:
                @pl.when(fro)
                def _():
                    face(m, dim, side).wait_recv()

    def sent_face(m, dim, only=None):
        for side, to, _ in sides(dim):
            if only is None or side == only:
                @pl.when(to)
                def _():
                    face(m, dim, side).wait_send()

    for dim in range(3):
        for side, _, fro in sides(dim):
            @pl.when(jnp.logical_not(fro))
            def _():
                if dim == 0:
                    p = 0 if side == 0 else NXL + 1
                    for t in range(STEPS):
                        A[t, :, p] = jnp.zeros((SOL, NYL, NZL), jnp.float32)
                    D[:, p] = jnp.zeros((SOL, NYL, NZL), jnp.float32)
                    if side == 0:
                        B[0] = jnp.zeros((NYL, NZL), jnp.float32)
                elif dim == 1:
                    for m in range(STEPS + 3):
                        yrcv[m, side] = jnp.zeros(yrcv.shape[2:], jnp.float32)
                else:
                    for m in range(STEPS + 3):
                        zrcv[m, side] = jnp.zeros(zrcv.shape[2:], jnp.float32)

    lane = lax.broadcasted_iota(jnp.int32, (NYL, NZL), 1)
    row = lax.broadcasted_iota(jnp.int32, (NYL, NZL), 0)
    first_row, last_row = row == 0, row == NYL - 1
    first_lane, last_lane = lane == 0, lane == NZL - 1

    def pack(packs, v, k):
        r = pltpu.roll(v, (k + 1) % NZL, 1)
        return jnp.where(lane == k, r, packs[0]), jnp.where(lane == k + 1, r, packs[1])

    def no_packs():
        return jnp.zeros((NYL, NZL), jnp.float32), jnp.zeros((NYL, NZL), jnp.float32)

    def y_pair(v, m, k):
        up = jnp.where(last_row, yrcv[m, 1, pl.ds(k, 1), :], pltpu.roll(v, NYL - 1, 0))
        dn = jnp.where(first_row, yrcv[m, 0, pl.ds(k, 1), :], pltpu.roll(v, 1, 0))
        return up, dn

    def z_pair(v, zr, k):
        up = jnp.where(last_lane, pltpu.roll(zr[1], (NZL - 2 - k) % NZL, 1), pltpu.roll(v, NZL - 1, 1))
        dn = jnp.where(first_lane, pltpu.roll(zr[0], (NZL - k) % NZL, 1), pltpu.roll(v, 1, 1))
        return up, dn

    for c in loads[:2]:
        c.wait()
    for m, src in ((0, A.at[0]), (DIF, D)):
        packs = no_packs()
        for s in range(SOL):
            for x in range(NXL):
                k = s * NXL + x
                v = src[s, x + 1]
                ysnd[m, 0, pl.ds(k, 1), :] = v[NYL - 1:, :]
                ysnd[m, 1, pl.ds(k, 1), :] = v[:1, :]
                packs = pack(packs, v, k)
        zsnd[m, 0], zsnd[m, 1] = packs

    pl.semaphore_wait(
        barrier, group - 1 + has_up[0].astype(jnp.int32) + has_dn[0].astype(jnp.int32)
    )

    def block(p, py, pz, slot):
        return pltpu.make_async_remote_copy(
            src_ref=vel_h.at[:, 0, pl.ds(pl.multiple_of(py * NYL, NYL), NYL), pl.ds(pl.multiple_of(pz * NZL, NZL), NZL)],
            dst_ref=V.at[:, slot],
            send_sem=vsend.at[p],
            recv_sem=vrecv.at[slot],
            device_id={"gy": py, "gz": pz},
            device_id_type=MESH,
        )

    @pl.loop(1, group)
    def _(o):
        py, pz, p = peer(o)
        block(p, py, pz, me).start()

    own = pltpu.make_async_copy(
        vel_h.at[:, 0, pl.ds(pl.multiple_of(place[1] * NYL, NYL), NYL), pl.ds(pl.multiple_of(place[2] * NZL, NZL), NZL)],
        V.at[:, me],
        vrecv.at[me],
    )
    own.start()
    for m in (0, DIF):
        for dim in range(3):
            send_face(m, dim)

    for c in loads[2:]:
        c.wait()
    own.wait()

    @pl.loop(1, group)
    def _(o):
        py, pz, p = peer(o)
        block(p, py, pz, p).wait_recv()

    def backward(c, x):
        v = step_scale * jnp.abs(V[c, x])
        return v * (1.0 - S[c, x].astype(jnp.float32))

    for x in reversed(range(NXL)):
        B[x + 1] = backward(0, x)
        if x == NXL - 1:
            send_face(BACK, 0, 0)
    zp = no_packs()
    for x in range(NXL):
        ysnd[BACK, 0, pl.ds(x, 1), :] = backward(1, x)[NYL - 1:, :]
        zp = pack(zp, backward(2, x), x)
    zsnd[BACK, 0] = zp[0]
    send_face(BACK, 1, 0)
    send_face(BACK, 2, 0)

    for dim in range(3):
        wait_face(DIF, dim)
    for dim in range(3):
        wait_face(BACK, dim, 0)

    up_y = jnp.logical_or(jnp.logical_not(last_row), has_up[1]).astype(jnp.float32)
    dn_y = jnp.logical_or(jnp.logical_not(first_row), has_dn[1]).astype(jnp.float32)
    up_z = jnp.logical_or(jnp.logical_not(last_lane), has_up[2]).astype(jnp.float32)
    dn_z = jnp.logical_or(jnp.logical_not(first_lane), has_dn[2]).astype(jnp.float32)
    up_x = jnp.where(has_up[0], 1.0, 0.0).astype(jnp.float32)
    dn_x = jnp.where(has_dn[0], 1.0, 0.0).astype(jnp.float32)

    zd = (zrcv[DIF, 0], zrcv[DIF, 1])
    zb = zrcv[BACK, 0]
    for x in range(NXL):
        keep = (1 - W[x]).astype(jnp.float32)
        forward, back = [], []
        for c in range(3):
            v = step_scale * jnp.abs(V[c, x])
            side = S[c, x].astype(jnp.float32)
            forward.append(v * side)
            back.append(v * (1.0 - side))
        below_x = B[x]
        below_y = jnp.where(first_row, yrcv[BACK, 0, pl.ds(x, 1), :], pltpu.roll(back[1], 1, 0))
        below_z = jnp.where(first_lane, pltpu.roll(zb, (NZL - x) % NZL, 1), pltpu.roll(back[2], 1, 1))
        for s in range(SOL):
            k = s * NXL + x
            d = D[s, x + 1]
            yu, yl = y_pair(d, DIF, k)
            zu, zl = z_pair(d, zd, k)
            c0 = forward[0] + half_scale * (d + D[s, x + 2])
            c1 = below_x + half_scale * (d + D[s, x])
            if x == NXL - 1:
                c0 = c0 * up_x
            if x == 0:
                c1 = c1 * dn_x
            c2 = up_y * (forward[1] + half_scale * (d + yu))
            c3 = dn_y * (below_y + half_scale * (d + yl))
            c4 = up_z * (forward[2] + half_scale * (d + zu))
            c5 = dn_z * (below_z + half_scale * (d + zl))
            K[s, x] = keep * (1.0 - (((c0 + c1) + (c2 + c3)) + (c4 + c5)))
            for i, c in enumerate((c0, c1, c2, c3, c4, c5)):
                C[i, s, x] = keep * c

    order = [0, NXL - 1] + list(range(1, NXL - 1))

    @pl.loop(0, STEPS)
    def _(t):
        for dim in range(3):
            wait_face(t, dim)
        zr = (zrcv[t, 0], zrcv[t, 1])
        packs = no_packs()
        for i, x in enumerate(order):
            for s in range(SOL):
                k = s * NXL + x
                a = A[t, s, x + 1]
                yu, yl = y_pair(a, t, k)
                zu, zl = z_pair(a, zr, k)
                new = (
                    (K[s, x] * a + C[0, s, x] * A[t, s, x + 2] + C[1, s, x] * A[t, s, x])
                    + (C[2, s, x] * yu + C[3, s, x] * yl)
                    + (C[4, s, x] * zu + C[5, s, x] * zl)
                )
                A[t + 1, s, x + 1] = new
                ysnd[t + 1, 0, pl.ds(k, 1), :] = new[NYL - 1:, :]
                ysnd[t + 1, 1, pl.ds(k, 1), :] = new[:1, :]
                packs = pack(packs, new, k)
            if i == 1:
                @pl.when(t < STEPS - 1)
                def _():
                    send_face(t + 1, 0)
        zsnd[t + 1, 0], zsnd[t + 1, 1] = packs

        @pl.when(t < STEPS - 1)
        def _():
            send_face(t + 1, 1)
            send_face(t + 1, 2)

    out = pltpu.make_async_copy(A.at[STEPS, :, pl.ds(1, NXL)], out_h, out_sem)
    out.start()
    for m in range(STEPS):
        for dim in range(3):
            sent_face(m, dim)
    for dim in range(3):
        sent_face(DIF, dim)
        sent_face(BACK, dim, 0)

    @pl.loop(1, group)
    def _(o):
        py, pz, p = peer(o)
        block(p, py, pz, me).wait_send()

    out.wait()


def solution(mesh):
    counts = tuple(mesh.shape[a] for a in AXES)

    def local(adjoint_final, velocity, diffusivity, upwind_side, wall_mask):
        dims = adjoint_final.shape
        sol, nxl, nyl, nzl = dims
        f32 = jnp.float32
        group = counts[1] * counts[2]
        messages = STEPS + 3
        return pl.pallas_call(
            functools.partial(kernel, dims, counts),
            out_shape=jax.ShapeDtypeStruct(dims, f32),
            in_specs=[pl.BlockSpec(memory_space=pl.ANY)] * 5,
            out_specs=pl.BlockSpec(memory_space=pl.ANY),
            scratch_shapes=[
                pltpu.VMEM((STEPS + 1, sol, nxl + 2, nyl, nzl), f32),
                pltpu.VMEM((3, nxl, nyl, nzl), f32),
                pltpu.VMEM((sol, nxl + 2, nyl, nzl), f32),
                pltpu.VMEM((3, nxl, nyl, nzl), jnp.int32),
                pltpu.VMEM((nxl, nyl, nzl), jnp.int32),
                pltpu.VMEM((nxl + 1, nyl, nzl), f32),
                pltpu.VMEM((6, sol, nxl, nyl, nzl), f32),
                pltpu.VMEM((sol, nxl, nyl, nzl), f32),
                pltpu.VMEM((messages, 2, sol * nxl, nzl), f32),
                pltpu.VMEM((messages, 2, sol * nxl, nzl), f32),
                pltpu.VMEM((messages, 2, nyl, nzl), f32),
                pltpu.VMEM((messages, 2, nyl, nzl), f32),
                pltpu.SemaphoreType.DMA((4,)),
                pltpu.SemaphoreType.DMA((group,)),
                pltpu.SemaphoreType.DMA((group,)),
                pltpu.SemaphoreType.DMA((messages, 3, 2)),
                pltpu.SemaphoreType.DMA((messages, 3, 2)),
                pltpu.SemaphoreType.DMA,
            ],
            compiler_params=pltpu.CompilerParams(
                collective_id=0, has_side_effects=True, vmem_limit_bytes=48 << 20
            ),
        )(adjoint_final, velocity, diffusivity, upwind_side, wall_mask)

    return jax.shard_map(
        local,
        mesh=mesh,
        in_specs=(
            P(None, "gx", "gy", "gz"),
            P(None, ("gx", "gy", "gz"), None, None),
            P(None, "gx", "gy", "gz"),
            P(None, "gx", "gy", "gz"),
            P("gx", "gy", "gz"),
        ),
        out_specs=P(None, "gx", "gy", "gz"),
        check_vma=False,
    )
```

time: 261 us -> 86.2 us (0.33)
  the two profiles are of different devices: /device:TPU:31 before, /device:TPU:28 now
where the time goes in v1:
time: 86.2 us; the launch traced here: 85.9 us
  Pallas kernels  80.2 us (93%)
  local copies, waits for them, and re-layouts  5.63 us (7%)
    pallas_call x1, Pallas kernels, local(): pl.pallas_call(functools.partial(kernel, dims, counts), out_shape=jax.Sha...  80.2 us
    unnamed x11, local copies, waits for them, and re-layouts  5.63 us

profile of v1, /device:TPU:28, one launch (start us, length us, event | category | flops | bytes accessed | tf_op | source)
XLA Modules:
  0.0 85.9 jit_solution(6769231696615755990)
XLA Ops:
  0.0 0.0 copy-start
  0.0 1.0 %copy-done = f32[3,32,8,128]{3,2,1,0:T(8,128)S(1)} copy-done((f32[3,32,8,128]{3,2,1,0:T(8,128)S(1)}, f32[3,32,8,128]{3,2,1,0:T(8,128)}, u32[]{:S(2)}) %copy-start) | copy-done | bytes 393240
  1.0 0.0 copy-start.1
  1.0 1.0 %copy-done.1 = f32[3,1,64,512]{3,2,1,0:T(8,128)S(1)} copy-done((f32[3,1,64,512]{3,2,1,0:T(8,128)S(1)}, f32[3,1,64,512]{3,2,1,0:T(8,128)}, u32[]{:S(2)}) %copy-start.1) | copy-done | bytes 393240
  2.0 0.0 copy-start.2
  2.0 1.0 %copy-done.2 = f32[3,32,8,128]{3,2,1,0:T(8,128)S(1)} copy-done((f32[3,32,8,128]{3,2,1,0:T(8,128)S(1)}, f32[3,32,8,128]{3,2,1,0:T(8,128)}, u32[]{:S(2)}) %copy-start.2) | copy-done | bytes 393240
  3.0 0.0 copy-start.3
  3.0 1.0 %copy-done.3 = s32[3,32,8,128]{3,2,1,0:T(8,128)S(1)} copy-done((s32[3,32,8,128]{3,2,1,0:T(8,128)S(1)}, s32[3,32,8,128]{3,2,1,0:T(8,128)}, u32[]{:S(2)}) %copy-start.3) | copy-done | bytes 393240
  4.0 0.0 copy-start.4
  4.0 0.9 %copy-done.4 = s32[32,8,128]{2,1,0:T(8,128)S(1)} copy-done((s32[32,8,128]{2,1,0:T(8,128)S(1)}, s32[32,8,128]{2,1,0:T(8,128)}, u32[]{:S(2)}) %copy-start.4) | copy-done | bytes 131096
  4.9 80.2 %shard_map.55 = f32[3,32,8,128]{3,2,1,0:T(8,128)S(1)} custom-call(f32[3,32,8,128]{3,2,1,0:T(8,128)S(1)} %copy-done, f32[3,1,64,512]{3,2,1,0:T(8,128)S(1)} %copy-done.1, f32[3,32,8,128]{3,2,1,0:T(8,128)S(1)} %copy-done.2, s32[3,32,8,128]{3,2,1,0:T(8,128)S(1)} %copy-done.3, s32[32,8,128]{2,1,0:T(8,128)S(1)} %copy-done.4), custom_call_target="tpu_custom_call" | custom-call | tf_op jit(solution)/shard_map/pallas_call | solution.py:315
  85.1 0.7 copy.7
Async XLA Ops:
  0.0 1.0 %copy-start = (f32[3,32,8,128]{3,2,1,0:T(8,128)S(1)}, f32[3,32,8,128]{3,2,1,0:T(8,128)}, u32[]{:S(2)}) copy-start(f32[3,32,8,128]{3,2,1,0:T(8,128)} %adj_h.1) | copy-start | bytes 1179652
  1.0 1.0 %copy-start.1 = (f32[3,1,64,512]{3,2,1,0:T(8,128)S(1)}, f32[3,1,64,512]{3,2,1,0:T(8,128)}, u32[]{:S(2)}) copy-start(f32[3,1,64,512]{3,2,1,0:T(8,128)} %vel_h.1) | copy-start | bytes 1179652
  2.0 1.0 %copy-start.2 = (f32[3,32,8,128]{3,2,1,0:T(8,128)S(1)}, f32[3,32,8,128]{3,2,1,0:T(8,128)}, u32[]{:S(2)}) copy-start(f32[3,32,8,128]{3,2,1,0:T(8,128)} %dif_h.1) | copy-start | bytes 1179652
  3.0 1.0 %copy-start.3 = (s32[3,32,8,128]{3,2,1,0:T(8,128)S(1)}, s32[3,32,8,128]{3,2,1,0:T(8,128)}, u32[]{:S(2)}) copy-start(s32[3,32,8,128]{3,2,1,0:T(8,128)} %side_h.1) | copy-start | bytes 1179652
  4.0 0.9 %copy-start.4 = (s32[32,8,128]{2,1,0:T(8,128)S(1)}, s32[32,8,128]{2,1,0:T(8,128)}, u32[]{:S(2)}) copy-start(s32[32,8,128]{2,1,0:T(8,128)} %wall_h.1) | copy-start | bytes 393220

commit v2 on v1

--- a/solution.py
+++ b/solution.py
@@ -10,7 +10,7 @@
 MESH = pl.DeviceIdType.MESH
 STEPS = 5
 AXES = ("gx", "gy", "gz")
-DIF, BACK = STEPS + 1, STEPS + 2
+DIF, BACK, COEF = STEPS + 1, STEPS + 2, STEPS + 3
 
 step_scale = 0.8
 half_scale = 0.4
@@ -19,8 +19,8 @@
 def kernel(
     dims, counts,
     adj_h, vel_h, dif_h, side_h, wall_h, out_h,
-    A, V, D, S, W, B, C, K, ysnd, yrcv, zsnd, zrcv,
-    load_sem, vsend, vrecv, fsend, frecv, out_sem,
+    A, V, D, S, W, B, C, K, ysnd, yrcv, zsnd, zrcv, late, edge_v,
+    load_sem, vsend, vrecv, esend, erecv, fsend, frecv, out_sem,
 ):
     SOL, NXL, NYL, NZL = dims
     ny, nz = counts[1], counts[2]
@@ -29,6 +29,10 @@
     has_up = [place[i] < counts[i] - 1 for i in range(3)]
     has_dn = [place[i] > 0 for i in range(3)]
     me = place[1] * nz + place[2]
+    half = ny // 2
+    far = (place[1] == half - 1, place[1] == half)
+    near_dn = jnp.logical_and(has_dn[1], jnp.logical_not(far[1]))
+    near_up = jnp.logical_and(has_up[1], jnp.logical_not(far[0]))
 
     loads = [
         pltpu.make_async_copy(adj_h, A.at[0, :, pl.ds(1, NXL)], load_sem.at[0]),
@@ -60,14 +64,14 @@
         to = {AXES[dim]: place[dim] + (1 - 2 * side)}
         if dim == 0:
             src_plane, dst_plane = (NXL, 0) if side == 0 else (1, NXL + 1)
-            if isinstance(m, int) and m == BACK:
+            if m == BACK:
                 src, dst = B.at[pl.ds(NXL, 1)], B.at[pl.ds(0, 1)]
-            elif isinstance(m, int) and m == DIF:
+            elif m == DIF:
                 src, dst = D.at[:, pl.ds(src_plane, 1)], D.at[:, pl.ds(dst_plane, 1)]
             else:
                 src, dst = A.at[m, :, pl.ds(src_plane, 1)], A.at[m, :, pl.ds(dst_plane, 1)]
         elif dim == 1:
-            if isinstance(m, int) and m == BACK:
+            if m == BACK:
                 src, dst = ysnd.at[m, side, pl.ds(0, NXL)], yrcv.at[m, side, pl.ds(0, NXL)]
             else:
                 src, dst = ysnd.at[m, side], yrcv.at[m, side]
@@ -77,7 +81,24 @@
             src_ref=src, dst_ref=dst, send_sem=send, recv_sem=recv, device_id=to, device_id_type=MESH
         )
 
+    def far_face(m, side):
+        src, dst = ysnd.at[m, side], late.at[m // 2] if m < STEPS and m % 2 else yrcv.at[m, side]
+        if m == BACK:
+            src, dst = src.at[pl.ds(0, NXL)], dst.at[pl.ds(0, NXL)]
+        return pltpu.make_async_remote_copy(
+            src_ref=src, dst_ref=dst, send_sem=fsend.at[m, 1, side], recv_sem=frecv.at[m, 1, side],
+            device_id={"gy": place[1] + (1 - 2 * side)}, device_id_type=MESH,
+        )
+
+    def both_far(act):
+        for side in (0, 1):
+            @pl.when(far[side])
+            def _():
+                act(side)
+
     def sides(dim):
+        if dim == 1:
+            return ((0, near_up, near_dn), (1, near_dn, near_up))
         return ((0, has_up[dim], has_dn[dim]), (1, has_dn[dim], has_up[dim]))
 
     def send_face(m, dim, only=None):
@@ -103,7 +124,9 @@
 
     for dim in range(3):
         for side, _, fro in sides(dim):
-            @pl.when(jnp.logical_not(fro))
+            outside = jnp.logical_not((has_dn, has_up)[side][dim])
+
+            @pl.when(outside)
             def _():
                 if dim == 0:
                     p = 0 if side == 0 else NXL + 1
@@ -113,11 +136,17 @@
                     if side == 0:
                         B[0] = jnp.zeros((NYL, NZL), jnp.float32)
                 elif dim == 1:
-                    for m in range(STEPS + 3):
+                    for m in range(STEPS + 4):
                         yrcv[m, side] = jnp.zeros(yrcv.shape[2:], jnp.float32)
                 else:
-                    for m in range(STEPS + 3):
+                    for m in range(STEPS + 4):
                         zrcv[m, side] = jnp.zeros(zrcv.shape[2:], jnp.float32)
+
+    def clear_late(side):
+        for m in range(1, STEPS, 2):
+            yrcv[m, 1 - side] = jnp.zeros(yrcv.shape[2:], jnp.float32)
+
+    both_far(clear_late)
 
     lane = lax.broadcasted_iota(jnp.int32, (NYL, NZL), 1)
     row = lax.broadcasted_iota(jnp.int32, (NYL, NZL), 0)
@@ -168,10 +197,34 @@
             device_id_type=MESH,
         )
 
+    def edge(p, pz, slot):
+        return pltpu.make_async_remote_copy(
+            src_ref=vel_h.at[1, 0, pl.ds((half - 1) * NYL, NYL), pl.ds(pl.multiple_of(pz * NZL, NZL), NZL)],
+            dst_ref=edge_v.at[slot],
+            send_sem=esend.at[p],
+            recv_sem=erecv.at[slot],
+            device_id={"gy": half, "gz": pz},
+            device_id_type=MESH,
+        )
+
     @pl.loop(1, group)
     def _(o):
         py, pz, p = peer(o)
         block(p, py, pz, me).start()
+
+        @pl.when(py == half)
+        def _():
+            edge(p, pz, me).start()
+
+    own_edge = pltpu.make_async_copy(
+        vel_h.at[1, 0, pl.ds((half - 1) * NYL, NYL), pl.ds(pl.multiple_of(place[2] * NZL, NZL), NZL)],
+        edge_v.at[me],
+        erecv.at[me],
+    )
+
+    @pl.when(far[1])
+    def _():
+        own_edge.start()
 
     own = pltpu.make_async_copy(
         vel_h.at[:, 0, pl.ds(pl.multiple_of(place[1] * NYL, NYL), NYL), pl.ds(pl.multiple_of(place[2] * NZL, NZL), NZL)],
@@ -182,10 +235,27 @@
     for m in (0, DIF):
         for dim in range(3):
             send_face(m, dim)
+        both_far(lambda side: far_face(m, side).start())
 
     for c in loads[2:]:
         c.wait()
+
+    @pl.when(far[0])
+    def _():
+        for x in range(NXL):
+            ysnd[BACK, 0, pl.ds(x, 1), :] = step_scale * (1.0 - S[1, x][NYL - 1:, :].astype(jnp.float32))
+        far_face(BACK, 0).start()
+
     own.wait()
+
+    @pl.when(far[1])
+    def _():
+        own_edge.wait()
+
+        @pl.loop(1, group)
+        def _(o):
+            py, pz, p = peer(o)
+            edge(p, pz, p).wait_recv()
 
     @pl.loop(1, group)
     def _(o):
@@ -202,16 +272,28 @@
             send_face(BACK, 0, 0)
     zp = no_packs()
     for x in range(NXL):
-        ysnd[BACK, 0, pl.ds(x, 1), :] = backward(1, x)[NYL - 1:, :]
         zp = pack(zp, backward(2, x), x)
     zsnd[BACK, 0] = zp[0]
+    send_face(BACK, 2, 0)
+
+    @pl.when(near_up)
+    def _():
+        for x in range(NXL):
+            ysnd[BACK, 0, pl.ds(x, 1), :] = backward(1, x)[NYL - 1:, :]
+
     send_face(BACK, 1, 0)
-    send_face(BACK, 2, 0)
 
     for dim in range(3):
         wait_face(DIF, dim)
+    both_far(lambda side: far_face(DIF, 1 - side).wait_recv())
     for dim in range(3):
         wait_face(BACK, dim, 0)
+
+    @pl.when(far[1])
+    def _():
+        far_face(BACK, 0).wait_recv()
+        for x in range(NXL):
+            yrcv[BACK, 0, pl.ds(x, 1), :] = yrcv[BACK, 0, pl.ds(x, 1), :] * jnp.abs(edge_v[x][NYL - 1:, :])
 
     up_y = jnp.logical_or(jnp.logical_not(last_row), has_up[1]).astype(jnp.float32)
     dn_y = jnp.logical_or(jnp.logical_not(first_row), has_dn[1]).astype(jnp.float32)
@@ -252,15 +334,30 @@
             for i, c in enumerate((c0, c1, c2, c3, c4, c5)):
                 C[i, s, x] = keep * c
 
-    order = [0, NXL - 1] + list(range(1, NXL - 1))
-
-    @pl.loop(0, STEPS)
-    def _(t):
+    def send_coef(side):
+        for k in range(SOL * NXL):
+            c = C[2 + side, k // NXL, k % NXL]
+            ysnd[COEF, side, pl.ds(k, 1), :] = c[NYL - 1:, :] if side == 0 else c[:1, :]
+        far_face(COEF, side).start()
+
+    both_far(send_coef)
+
+    for t in range(STEPS):
         for dim in range(3):
             wait_face(t, dim)
+
+        if t % 2 == 0:
+            def arrived(side):
+                far_face(t, 1 - side).wait_recv()
+                if t == 2:
+                    far_face(COEF, 1 - side).wait_recv()
+                if t > 0:
+                    yrcv[t, 1 - side] = yrcv[t, 1 - side] + yrcv[COEF, 1 - side] * ysnd[t - 1, side]
+
+            both_far(arrived)
+
         zr = (zrcv[t, 0], zrcv[t, 1])
-        packs = no_packs()
-        for i, x in enumerate(order):
+        for x in range(NXL):
             for s in range(SOL):
                 k = s * NXL + x
                 a = A[t, s, x + 1]
@@ -274,16 +371,28 @@
                 A[t + 1, s, x + 1] = new
                 ysnd[t + 1, 0, pl.ds(k, 1), :] = new[NYL - 1:, :]
                 ysnd[t + 1, 1, pl.ds(k, 1), :] = new[:1, :]
-                packs = pack(packs, new, k)
-            if i == 1:
-                @pl.when(t < STEPS - 1)
-                def _():
-                    send_face(t + 1, 0)
-        zsnd[t + 1, 0], zsnd[t + 1, 1] = packs
-
-        @pl.when(t < STEPS - 1)
-        def _():
+
+        if t % 2:
+            def finish(side):
+                if t < STEPS - 1:
+                    far_face(t + 1, side).start()
+                far_face(t, 1 - side).wait_recv()
+                rows = ysnd[t + 1, side] + ysnd[COEF, side] * late[t // 2]
+                r = NYL - 1 if side == 0 else 0
+                for k in range(SOL * NXL):
+                    A[t + 1, k // NXL, k % NXL + 1, pl.ds(r, 1), :] = rows[k:k + 1, :]
+
+            both_far(finish)
+
+        if t < STEPS - 1:
+            send_face(t + 1, 0)
             send_face(t + 1, 1)
+            if t % 2 == 0:
+                both_far(lambda side: far_face(t + 1, side).start())
+            packs = no_packs()
+            for k in range(SOL * NXL):
+                packs = pack(packs, A[t + 1, k // NXL, k % NXL + 1], k)
+            zsnd[t + 1, 0], zsnd[t + 1, 1] = packs
             send_face(t + 1, 2)
 
     out = pltpu.make_async_copy(A.at[STEPS, :, pl.ds(1, NXL)], out_h, out_sem)
@@ -295,10 +404,22 @@
         sent_face(DIF, dim)
         sent_face(BACK, dim, 0)
 
+    def sent_far(side):
+        for m in list(range(STEPS)) + [DIF, COEF]:
+            far_face(m, side).wait_send()
+        if side == 0:
+            far_face(BACK, side).wait_send()
+
+    both_far(sent_far)
+
     @pl.loop(1, group)
     def _(o):
         py, pz, p = peer(o)
         block(p, py, pz, me).wait_send()
+
+        @pl.when(py == half)
+        def _():
+            edge(p, pz, me).wait_send()
 
     out.wait()
 
@@ -311,7 +432,7 @@
         sol, nxl, nyl, nzl = dims
         f32 = jnp.float32
         group = counts[1] * counts[2]
-        messages = STEPS + 3
+        messages = STEPS + 4
         return pl.pallas_call(
             functools.partial(kernel, dims, counts),
             out_shape=jax.ShapeDtypeStruct(dims, f32),
@@ -330,7 +451,11 @@
                 pltpu.VMEM((messages, 2, sol * nxl, nzl), f32),
                 pltpu.VMEM((messages, 2, nyl, nzl), f32),
                 pltpu.VMEM((messages, 2, nyl, nzl), f32),
+                pltpu.VMEM((STEPS // 2, sol * nxl, nzl), f32),
+                pltpu.VMEM((group, nyl, nzl), f32),
                 pltpu.SemaphoreType.DMA((4,)),
+                pltpu.SemaphoreType.DMA((group,)),
+                pltpu.SemaphoreType.DMA((group,)),
                 pltpu.SemaphoreType.DMA((group,)),
                 pltpu.SemaphoreType.DMA((group,)),
                 pltpu.SemaphoreType.DMA((messages, 3, 2)),
@@ -338,7 +463,7 @@
                 pltpu.SemaphoreType.DMA,
             ],
             compiler_params=pltpu.CompilerParams(
-                collective_id=0, has_side_effects=True, vmem_limit_bytes=48 << 20
+                collective_id=0, has_side_effects=True, vmem_limit_bytes=62 << 20
             ),
         )(adjoint_final, velocity, diffusivity, upwind_side, wall_mask)
 

time: 86.2 us -> 57.7 us (0.67)
  the two profiles are of different devices: /device:TPU:28 before, /device:TPU:31 now
where the time goes in v2:
time: 57.7 us; the launch traced here: 57.5 us
  Pallas kernels  55.8 us (97%)
  local copies, waits for them, and re-layouts  1.77 us (3%)
    pallas_call x1, Pallas kernels, local(): pl.pallas_call(functools.partial(kernel, dims, counts), out_shape=jax.Sha...  55.8 us
    unnamed x1, local copies, waits for them, and re-layouts  1.77 us

profile of v2, /device:TPU:31, one launch (start us, length us, event | category | flops | bytes accessed | tf_op | source)
XLA Modules:
  0.0 57.5 jit_solution(11652479261319496319)
XLA Ops:
  0.0 55.8 %shard_map.55 = f32[3,32,8,128]{3,2,1,0:T(8,128)} custom-call(f32[3,32,8,128]{3,2,1,0:T(8,128)} %adj_h.1, f32[3,1,64,512]{3,2,1,0:T(8,128)} %vel_h.1, f32[3,32,8,128]{3,2,1,0:T(8,128)} %dif_h.1, s32[3,32,8,128]{3,2,1,0:T(8,128)} %side_h.1, s32[32,8,128]{2,1,0:T(8,128)} %wall_h.1), custom_call_target="tpu_custom_call" | custom-call | tf_op jit(solution)/shard_map/pallas_call | solution.py:436
  55.8 1.8 %copy.7 = f32[3,32,8,128]{3,2,1,0:T(8,128)} copy(f32[3,32,8,128]{3,2,1,0:T(8,128)} %shard_map.55) | data formatting | bytes 786432

commit v3 on v2

--- a/solution.py
+++ b/solution.py
@@ -9,6 +9,7 @@
 
 MESH = pl.DeviceIdType.MESH
 STEPS = 5
+PARTS = 4
 AXES = ("gx", "gy", "gz")
 DIF, BACK, COEF = STEPS + 1, STEPS + 2, STEPS + 3
 
@@ -209,7 +210,10 @@
 
     @pl.loop(1, group)
     def _(o):
-        py, pz, p = peer(o)
+        x, z = lax.rem(place[1], half), (place[1] // half) * nz + place[2]
+        x, z = lax.rem(x + o // (2 * nz), half), lax.rem(z + o * 3, 2 * nz)
+        py, pz = (z // nz) * half + x, lax.rem(z, nz)
+        p = py * nz + pz
         block(p, py, pz, me).start()
 
         @pl.when(py == half)
@@ -232,9 +236,7 @@
         vrecv.at[me],
     )
     own.start()
-    for m in (0, DIF):
-        for dim in range(3):
-            send_face(m, dim)
+    for m in (DIF, 0):
         both_far(lambda side: far_face(m, side).start())
 
     for c in loads[2:]:
@@ -245,6 +247,10 @@
         for x in range(NXL):
             ysnd[BACK, 0, pl.ds(x, 1), :] = step_scale * (1.0 - S[1, x][NYL - 1:, :].astype(jnp.float32))
         far_face(BACK, 0).start()
+
+    for m in (DIF, 0):
+        for dim in range(3):
+            send_face(m, dim)
 
     own.wait()
 
@@ -334,13 +340,19 @@
             for i, c in enumerate((c0, c1, c2, c3, c4, c5)):
                 C[i, s, x] = keep * c
 
-    def send_coef(side):
+    def pack_coef(side):
         for k in range(SOL * NXL):
             c = C[2 + side, k // NXL, k % NXL]
             ysnd[COEF, side, pl.ds(k, 1), :] = c[NYL - 1:, :] if side == 0 else c[:1, :]
-        far_face(COEF, side).start()
-
-    both_far(send_coef)
+
+    both_far(pack_coef)
+
+    PART = NXL // PARTS
+
+    def out_copy(part):
+        return pltpu.make_async_copy(
+            A.at[STEPS, :, pl.ds(1 + part * PART, PART)], out_h.at[:, pl.ds(part * PART, PART)], out_sem.at[part]
+        )
 
     for t in range(STEPS):
         for dim in range(3):
@@ -369,34 +381,38 @@
                     + (C[4, s, x] * zu + C[5, s, x] * zl)
                 )
                 A[t + 1, s, x + 1] = new
-                ysnd[t + 1, 0, pl.ds(k, 1), :] = new[NYL - 1:, :]
-                ysnd[t + 1, 1, pl.ds(k, 1), :] = new[:1, :]
+                if t < STEPS - 1:
+                    ysnd[t + 1, 0, pl.ds(k, 1), :] = new[NYL - 1:, :]
+                    ysnd[t + 1, 1, pl.ds(k, 1), :] = new[:1, :]
+            if t == STEPS - 1 and (x + 1) % PART == 0:
+                out_copy(x // PART).start()
 
         if t % 2:
             def finish(side):
-                if t < STEPS - 1:
-                    far_face(t + 1, side).start()
                 far_face(t, 1 - side).wait_recv()
                 rows = ysnd[t + 1, side] + ysnd[COEF, side] * late[t // 2]
                 r = NYL - 1 if side == 0 else 0
                 for k in range(SOL * NXL):
                     A[t + 1, k // NXL, k % NXL + 1, pl.ds(r, 1), :] = rows[k:k + 1, :]
 
+            both_far(lambda side: far_face(t + 1, side).start())
+            send_face(t + 1, 1)
             both_far(finish)
 
         if t < STEPS - 1:
-            send_face(t + 1, 0)
-            send_face(t + 1, 1)
             if t % 2 == 0:
                 both_far(lambda side: far_face(t + 1, side).start())
+            send_face(t + 1, 0)
+            if t % 2 == 0:
+                send_face(t + 1, 1)
             packs = no_packs()
             for k in range(SOL * NXL):
                 packs = pack(packs, A[t + 1, k // NXL, k % NXL + 1], k)
             zsnd[t + 1, 0], zsnd[t + 1, 1] = packs
             send_face(t + 1, 2)
-
-    out = pltpu.make_async_copy(A.at[STEPS, :, pl.ds(1, NXL)], out_h, out_sem)
-    out.start()
+            if t == 0:
+                both_far(lambda side: far_face(COEF, side).start())
+
     for m in range(STEPS):
         for dim in range(3):
             sent_face(m, dim)
@@ -421,7 +437,8 @@
         def _():
             edge(p, pz, me).wait_send()
 
-    out.wait()
+    for part in range(PARTS):
+        out_copy(part).wait()
 
 
 def solution(mesh):
@@ -460,7 +477,7 @@
                 pltpu.SemaphoreType.DMA((group,)),
                 pltpu.SemaphoreType.DMA((messages, 3, 2)),
                 pltpu.SemaphoreType.DMA((messages, 3, 2)),
-                pltpu.SemaphoreType.DMA,
+                pltpu.SemaphoreType.DMA((PARTS,)),
             ],
             compiler_params=pltpu.CompilerParams(
                 collective_id=0, has_side_effects=True, vmem_limit_bytes=62 << 20

time: 57.7 us -> 56.6 us (0.981)
  Pallas kernels: 55.8 us -> 54.6 us
    pallas_call x1, Pallas kernels: 55.8 us -> 54.6 us  [local(): pl.pallas_call(functools.partial(kernel, dims, counts), out_shape=jax.Sha...]
where the time goes in v3:
time: 56.6 us; the launch traced here: 56.4 us
  Pallas kernels  54.6 us (96%)
  local copies, waits for them, and re-layouts  1.77 us (3%)
    pallas_call x1, Pallas kernels, local(): pl.pallas_call(functools.partial(kernel, dims, counts), out_shape=jax.Sha...  54.6 us
    unnamed x1, local copies, waits for them, and re-layouts  1.77 us

profile of v3, /device:TPU:31, one launch (start us, length us, event | category | flops | bytes accessed | tf_op | source)
XLA Modules:
  0.0 56.4 jit_solution(11628782506328715360)
XLA Ops:
  0.0 54.6 %shard_map.55 = f32[3,32,8,128]{3,2,1,0:T(8,128)} custom-call(f32[3,32,8,128]{3,2,1,0:T(8,128)} %adj_h.1, f32[3,1,64,512]{3,2,1,0:T(8,128)} %vel_h.1, f32[3,32,8,128]{3,2,1,0:T(8,128)} %dif_h.1, s32[3,32,8,128]{3,2,1,0:T(8,128)} %side_h.1, s32[32,8,128]{2,1,0:T(8,128)} %wall_h.1), custom_call_target="tpu_custom_call" | custom-call | tf_op jit(solution)/shard_map/pallas_call | solution.py:453
  54.6 1.8 %copy.7 = f32[3,32,8,128]{3,2,1,0:T(8,128)} copy(f32[3,32,8,128]{3,2,1,0:T(8,128)} %shard_map.55) | data formatting | bytes 786432
